TPU v7x, 128 devices: a whole 4x4x4 slice. The times are simulated.
128 devices in a mesh: row: 16 (over y, x), col: 8 (over z, core).
Axes of the slice: x: 4, y: 4, z: 4, core: 2. Of those that a mesh axis runs over, the one named last changes fastest.
Arguments:
- inputs: bfloat16 [1024, 8192], P('col', 'row'), may hold values from -6 to 6
- out_grad: bfloat16 [1024, 8192], P('col', 'row'), may hold values from -1.5 to 1.5
- gate_pre: bfloat16 [1024, 14336], P('row', 'col'), may hold values from -9 to 9
- up_pre: bfloat16 [1024, 14336], P('row', 'col'), may hold values from -6 to 6
- gate_weight: bfloat16 [8192, 14336], P('row', 'col'), may hold values from -0.0625 to 0.0625
- up_weight: bfloat16 [8192, 14336], P('row', 'col'), may hold values from -0.0625 to 0.0625
- down_weight: bfloat16 [14336, 8192], P('col', 'row'), may hold values from -0.046875 to 0.046875
Outputs:
- input_grad: float32 [1024, 8192], P('col', 'row')
- gate_grad: float32 [8192, 14336], P('row', 'col')
- up_grad: float32 [8192, 14336], P('row', 'col')
- down_grad: float32 [14336, 8192], P('col', 'row')
All inputs are finite; a program needn't handle non-finite values.
Results may differ from a plain program's by a relative error of at most 0.0029.
Values may be sent and summed in bfloat16 or wider, within the bound.
A program may use at most 128 MiB of HBM per device.

v0:
```python
import jax
import jax.numpy as jnp
from jax import lax
from jax.sharding import PartitionSpec as P

LEAD_DIMS = (((0,), (0,)), ((), ()))
LAST_DIMS = (((1,), (1,)), ((), ()))


def body(inputs, out_grad, gate_pre, up_pre, gate_weight, up_weight, down_weight):
    gate_val = gate_pre.astype(jnp.float32)
    up_val = up_pre.astype(jnp.float32)
    gate_sig = jax.nn.sigmoid(gate_val)
    hidden = (gate_val * gate_sig * up_val).astype(jnp.bfloat16)
    grad_full = lax.all_gather(out_grad, "col", axis=0, tiled=True)
    hidden_all = lax.all_gather(hidden, "row", axis=0, tiled=True)
    partial_sum = lax.dot_general(
        grad_full, down_weight, LAST_DIMS, preferred_element_type=jnp.float32
    )
    grad_hidden = lax.psum_scatter(partial_sum, "row", scatter_dimension=0, tiled=True)
    input_full = lax.all_gather(inputs, "col", axis=0, tiled=True)
    grad_gate = (grad_hidden * up_val * gate_sig * (1.0 + gate_val * (1.0 - gate_sig))).astype(
        jnp.bfloat16
    )
    grad_up = (grad_hidden * gate_val * gate_sig).astype(jnp.bfloat16)
    down_grad = lax.dot_general(
        hidden_all, grad_full, LEAD_DIMS, preferred_element_type=jnp.float32
    )
    gate_all = lax.all_gather(grad_gate, "row", axis=0, tiled=True)
    up_all = lax.all_gather(grad_up, "row", axis=0, tiled=True)
    total = lax.dot_general(gate_all, gate_weight, LAST_DIMS, preferred_element_type=jnp.float32)
    input_grad = lax.psum_scatter(
        total + lax.dot_general(up_all, up_weight, LAST_DIMS, preferred_element_type=jnp.float32),
        "col",
        scatter_dimension=0,
        tiled=True,
    )
    gate_grad = lax.dot_general(input_full, gate_all, LEAD_DIMS, preferred_element_type=jnp.float32)
    up_grad = lax.dot_general(input_full, up_all, LEAD_DIMS, preferred_element_type=jnp.float32)
    return (input_grad, gate_grad, up_grad, down_grad)


def solution(mesh):
    in_specs = (
        P("col", "row"),
        P("col", "row"),
        P("row", "col"),
        P("row", "col"),
        P("row", "col"),
        P("row", "col"),
        P("col", "row"),
    )
    out_specs = (P("col", "row"), P("row", "col"), P("row", "col"), P("col", "row"))
    return jax.shard_map(body, mesh=mesh, in_specs=in_specs, out_specs=out_specs, check_vma=False)
```

profile of v0, /device:TPU:0, one launch (start us, length us, event | category | flops | bytes accessed | tf_op | source)
XLA Modules:
  0.0 347.5 jit_solution(18138531377756682958)
XLA Ops:
  7.2 0.7 all-gather.6.cloned.1.call-update
  7.9 0.0 reduce-scatter.3.cloned.1.call-start
  8.0 27.8 %all-gather.6.cloned.1.call-done = bf16[1024,512]{1,0:T(8,128)(2,1)} async-done(((bf16[128,512]{1,0:T(8,128)(2,1)}), bf16[1024,512]{1,0:T(8,128)(2,1)}) %all-gather.6.cloned.1.call-update) | async-done | bytes 1048592 | tf_op jit(solution)/shard_map/all_gather | solution.py:15
  35.8 6.3 %fusion.10 = f32[1024,1792]{1,0:T(8,128)} fusion(bf16[1024,512]{1,0:T(8,128)(2,1)} %all-gather.6.cloned.1.call-done, bf16[1792,512]{1,0:T(8,128)(2,1)S(1)} %copy-done), kind=kOutput, calls=%fused_computation.19 | convolution fusion | flops 1879048192 | bytes 10223616 | tf_op jit(solution)/shard_map/dot_general | solution.py:17
  42.1 0.0 all-gather.8.cloned.1.call-start
  42.2 82.8 %reduce-scatter.3.cloned.1.call-done = f32[64,1792]{1,0:T(8,128)} async-done(((f32[1024,1792]{1,0:T(8,128)}), f32[64,1792]{1,0:T(8,128)}) %reduce-scatter.3.cloned.1.call-update) | async-done | bytes 458768 | tf_op jit(solution)/shard_map/reduce_scatter | solution.py:20
  124.9 2.1 fusion.9
  127.0 0.0 all-gather.10.cloned.1.call-start
  127.1 0.5 all-gather.10.cloned.1.call-update
  127.7 0.5 all-gather.12.cloned.1.call-update
  128.2 0.5 all-gather.14.cloned.1.call-update
  128.8 0.0 reduce-scatter.5.cloned.1.call-start
  128.8 47.9 %all-gather.8.cloned.1.call-done = bf16[1024,1792]{1,0:T(8,128)(2,1)} async-done(((bf16[64,1792]{1,0:T(8,128)(2,1)}), bf16[1024,1792]{1,0:T(8,128)(2,1)}) %all-gather.8.cloned.1.call-update) | async-done | bytes 3670032 | tf_op jit(solution)/shard_map/all_gather | solution.py:29
  176.7 6.0 %fusion.11 = f32[1024,512]{1,0:T(8,128)} fusion(bf16[1024,1792]{1,0:T(8,128)(2,1)} %all-gather.8.cloned.1.call-done, bf16[512,1792]{1,0:T(8,128)(2,1)} %param.11), kind=kOutput, calls=%fused_computation.20 | convolution fusion | flops 1879048192 | bytes 7602176 | tf_op jit(solution)/shard_map/dot_general | solution.py:31
  182.8 45.6 %all-gather.10.cloned.1.call-done = bf16[1024,1792]{1,0:T(8,128)(2,1)} async-done(((bf16[64,1792]{1,0:T(8,128)(2,1)}), bf16[1024,1792]{1,0:T(8,128)(2,1)}) %all-gather.10.cloned.1.call-update) | async-done | bytes 3670032 | tf_op jit(solution)/shard_map/all_gather | solution.py:30
  228.3 6.7 %convolution_add_fusion = f32[1024,512]{1,0:T(8,128)} fusion(f32[1024,512]{1,0:T(8,128)} %fusion.11, bf16[1024,1792]{1,0:T(8,128)(2,1)} %all-gather.10.cloned.1.call-done, bf16[512,1792]{1,0:T(8,128)(2,1)} %param.12), kind=kOutput, calls=%fused_computation.2 | convolution fusion | flops 1879572480 | bytes 9699328 | tf_op jit(solution)/shard_map/dot_general | solution.py:33
  235.1 17.7 %all-gather.12.cloned.1.call-done = bf16[1024,512]{1,0:T(8,128)(2,1)} async-done(((bf16[128,512]{1,0:T(8,128)(2,1)}), bf16[1024,512]{1,0:T(8,128)(2,1)}) %all-gather.12.cloned.1.call-update) | async-done | bytes 1048592 | tf_op jit(solution)/shard_map/all_gather | solution.py:21
  252.8 6.3 %convolution_bitcast_fusion.1 = f32[512,1792]{0,1:T(8,128)} fusion(bf16[1024,1792]{1,0:T(8,128)(2,1)} %all-gather.8.cloned.1.call-done, bf16[1024,512]{1,0:T(8,128)(2,1)} %all-gather.12.cloned.1.call-done), kind=kOutput, calls=%fused_computation.1 | convolution fusion | flops 1879048192 | bytes 8388608 | tf_op jit(solution)/shard_map/dot_general | solution.py:38
  259.1 5.2 %copy.11 = f32[512,1792]{1,0:T(8,128)} copy(f32[512,1792]{0,1:T(8,128)} %convolution_bitcast_fusion.1) | data formatting | bytes 7340032
  264.3 6.1 %convolution_bitcast_fusion = f32[512,1792]{0,1:T(8,128)} fusion(bf16[1024,1792]{1,0:T(8,128)(2,1)} %all-gather.10.cloned.1.call-done, bf16[1024,512]{1,0:T(8,128)(2,1)S(1)} %copy-done.4), kind=kOutput, calls=%fused_computation | convolution fusion | flops 1879048192 | bytes 8388608 | tf_op jit(solution)/shard_map/dot_general | solution.py:39
  270.4 5.2 %copy.12 = f32[512,1792]{1,0:T(8,128)} copy(f32[512,1792]{0,1:T(8,128)} %convolution_bitcast_fusion) | data formatting | bytes 7340032
  275.7 28.9 %all-gather.14.cloned.1.call-done = bf16[1024,1792]{1,0:T(8,128)(2,1)} async-done(((bf16[64,1792]{1,0:T(8,128)(2,1)}), bf16[1024,1792]{1,0:T(8,128)(2,1)}) %all-gather.14.cloned.1.call-update) | async-done | bytes 3670032 | tf_op jit(solution)/shard_map/all_gather | solution.py:16
  304.5 6.0 %fusion.12 = f32[1792,512]{1,0:T(8,128)} fusion(bf16[1024,1792]{1,0:T(8,128)(2,1)} %all-gather.14.cloned.1.call-done, bf16[1024,512]{1,0:T(8,128)(2,1)S(1)} %copy-done.3), kind=kOutput, calls=%fused_computation.21 | convolution fusion | flops 1879048192 | bytes 8388608 | tf_op jit(solution)/shard_map/dot_general | solution.py:26
  310.5 30.2 %reduce-scatter.5.cloned.1.call-done = f32[128,512]{1,0:T(8,128)} async-done(((f32[1024,512]{1,0:T(8,128)}), f32[128,512]{1,0:T(8,128)}) %reduce-scatter.5.cloned.1.call-update) | async-done | bytes 262160 | tf_op jit(solution)/shard_map/reduce_scatter | solution.py:32
  (16 shorter events, 0.2 us)
Async XLA Ops:
  7.2 28.6 %copy-start = (bf16[1792,512]{1,0:T(8,128)(2,1)S(1)}, bf16[1792,512]{1,0:T(8,128)(2,1)}, u32[]{:S(2)}) copy-start(bf16[1792,512]{1,0:T(8,128)(2,1)} %param.13) | copy-start | bytes 5505028
  7.2 28.6 %all-gather.6.cloned.1.call-start = ((), (), s32[]{:S(2)}) async-start(), calls=%async_computation.2 | async-start | bytes 1179648 | tf_op jit(solution)/shard_map/all_gather | solution.py:15
  7.9 117.0 %reduce-scatter.3.cloned.1.call-start = ((), (), s32[]{:S(2)}) async-start(), calls=%async_computation.3 | async-start | bytes 7798784 | tf_op jit(solution)/shard_map/reduce_scatter | solution.py:20
  42.1 82.8 %copy-start.1 = (bf16[64,1792]{1,0:T(8,128)(2,1)S(1)}, bf16[64,1792]{1,0:T(8,128)(2,1)}, u32[]{:S(2)}) copy-start(bf16[64,1792]{1,0:T(8,128)(2,1)} %param.9) | copy-start | bytes 688132
  42.1 82.8 %copy-start.2 = (bf16[64,1792]{1,0:T(8,128)(2,1)S(1)}, bf16[64,1792]{1,0:T(8,128)(2,1)}, u32[]{:S(2)}) copy-start(bf16[64,1792]{1,0:T(8,128)(2,1)} %param.10) | copy-start | bytes 688132
  42.1 134.6 %all-gather.8.cloned.1.call-start = ((), (), s32[]{:S(2)}) async-start(), calls=%async_computation.4 | async-start | bytes 3899392 | tf_op jit(solution)/shard_map/all_gather | solution.py:29
  127.0 101.3 %all-gather.10.cloned.1.call-start = ((), (), s32[]{:S(2)}) async-start(), calls=%async_computation.5 | async-start | bytes 3899392 | tf_op jit(solution)/shard_map/all_gather | solution.py:30
  127.6 125.2 %all-gather.12.cloned.1.call-start = ((), (), s32[]{:S(2)}) async-start(), calls=%async_computation.7 | async-start | bytes 1179648 | tf_op jit(solution)/shard_map/all_gather | solution.py:21
  128.2 176.3 %all-gather.14.cloned.1.call-start = ((), (), s32[]{:S(2)}) async-start(), calls=%async_computation.8 | async-start | bytes 3899392 | tf_op jit(solution)/shard_map/all_gather | solution.py:16
  128.8 211.9 %reduce-scatter.5.cloned.1.call-start = ((), (), s32[]{:S(2)}) async-start(), calls=%async_computation.6 | async-start | bytes 2359296 | tf_op jit(solution)/shard_map/reduce_scatter | solution.py:32
  259.1 5.2 %copy-start.4 = (bf16[1024,512]{1,0:T(8,128)(2,1)S(1)}, bf16[1024,512]{1,0:T(8,128)(2,1)}, u32[]{:S(2)}) copy-start(bf16[1024,512]{1,0:T(8,128)(2,1)} %all-gather.12.cloned.1.call-done) | copy-start | bytes 3145732
  270.4 34.1 %copy-start.3 = (bf16[1024,512]{1,0:T(8,128)(2,1)S(1)}, bf16[1024,512]{1,0:T(8,128)(2,1)}, u32[]{:S(2)}) copy-start(bf16[1024,512]{1,0:T(8,128)(2,1)} %all-gather.6.cloned.1.call-done) | copy-start | bytes 3145732
Sparse Core Ops, SparseCore 0:
  9.7 26.0 all-gather.5
  42.2 82.6 reduce-scatter.2
  127.9 48.8 all-gather.7
  179.5 48.7 all-gather.9
  230.0 22.7 all-gather.11
  255.1 49.4 all-gather.13
  307.6 32.9 reduce-scatter.4
where the time goes:
time: 348 us; the launch traced here: 347 us
  waiting for transfers between devices  283 us (81%)
  matrix products  37.4 us (11%)
  between operations  14.1 us (4%)
  local copies, waits for them, and re-layouts  10.5 us (3%)
    reduce_scatter x1, waiting for transfers between devices, body(): lax.psum_scatter(partial_sum, 'row', scatter_dimension=0, tiled=True)  82.8 us
    all_gather x1, waiting for transfers between devices, body(): gate_all = lax.all_gather(grad_gate, 'row', axis=0, tiled=True)  47.9 us
    all_gather x1, waiting for transfers between devices, body(): up_all = lax.all_gather(grad_up, 'row', axis=0, tiled=True)  45.6 us
    reduce_scatter x1, waiting for transfers between devices, body(): lax.psum_scatter(total + lax.dot_general(up_all, up_weight, LAST_DIMS, pr...  30.2 us
    all_gather x1, waiting for transfers between devices, body(): hidden_all = lax.all_gather(hidden, 'row', axis=0, tiled=True)  28.9 us
    all_gather x1, waiting for transfers between devices, body(): grad_full = lax.all_gather(out_grad, 'col', axis=0, tiled=True)  27.8 us
    all_gather x1, waiting for transfers between devices, body(): input_full = lax.all_gather(inputs, 'col', axis=0, tiled=True)  17.7 us
    unnamed x12, local copies, waits for them, and re-layouts  10.5 us
  transfers between devices with their start and end apart: 7, of which 7 were waited for; matrix products, arithmetic and copies ran while one was open for 12% of the time, Pallas kernels for 0%

commit v1 on v0

--- a/solution.py
+++ b/solution.py
@@ -26,8 +26,11 @@
     down_grad = lax.dot_general(
         hidden_all, grad_full, LEAD_DIMS, preferred_element_type=jnp.float32
     )
-    gate_all = lax.all_gather(grad_gate, "row", axis=0, tiled=True)
-    up_all = lax.all_gather(grad_up, "row", axis=0, tiled=True)
+    gate_all, up_all = jnp.split(
+        lax.all_gather(jnp.concatenate([grad_gate, grad_up], axis=1), "row", axis=0, tiled=True),
+        [grad_gate.shape[1]],
+        axis=1,
+    )
     total = lax.dot_general(gate_all, gate_weight, LAST_DIMS, preferred_element_type=jnp.float32)
     input_grad = lax.psum_scatter(
         total + lax.dot_general(up_all, up_weight, LAST_DIMS, preferred_element_type=jnp.float32),

time: 348 us -> 314 us (0.902)
  waiting for transfers between devices: 283 us -> 253 us
  matrix products: 37.4 us -> 32.9 us
    all_gather x2 -> x1, waiting for transfers between devices: 93.5 us -> 64.3 us  [body(): lax.all_gather(jnp.concatenate([grad_gate, grad_up], axis=1), 'row', axis...]
    reduce_scatter x1, waiting for transfers between devices: 30.2 us -> 14.1 us  [body(): lax.psum_scatter(total + lax.dot_general(up_all, up_weight, LAST_DIMS, pr...]
    all_gather x1, waiting for transfers between devices: 28.9 us -> 43.3 us  [body(): hidden_all = lax.all_gather(hidden, 'row', axis=0, tiled=True)]
    unnamed x12 -> x16, local copies, waits for them, and re-layouts: 10.5 us -> 10.8 us
  transfers between devices with their start and end apart: 7 -> 6, of which waited for: 7 -> 6; matrix products, arithmetic and copies ran while one was open for 12% -> 12% of each run, Pallas kernels for 0% -> 0%
where the time goes in v1:
time: 314 us; the launch traced here: 313 us
  waiting for transfers between devices  253 us (81%)
  matrix products  32.9 us (10%)
  between operations  14.1 us (4%)
  local copies, waits for them, and re-layouts  10.8 us (3%)
    reduce_scatter x1, waiting for transfers between devices, body(): lax.psum_scatter(partial_sum, 'row', scatter_dimension=0, tiled=True)  82.8 us
    all_gather x1, waiting for transfers between devices, body(): lax.all_gather(jnp.concatenate([grad_gate, grad_up], axis=1), 'row', axis...  64.3 us
    all_gather x1, waiting for transfers between devices, body(): hidden_all = lax.all_gather(hidden, 'row', axis=0, tiled=True)  43.3 us
    all_gather x1, waiting for transfers between devices, body(): grad_full = lax.all_gather(out_grad, 'col', axis=0, tiled=True)  27.8 us
    all_gather x1, waiting for transfers between devices, body(): input_full = lax.all_gather(inputs, 'col', axis=0, tiled=True)  18.5 us
    reduce_scatter x1, waiting for transfers between devices, body(): lax.psum_scatter(total + lax.dot_general(up_all, up_weight, LAST_DIMS, pr...  14.1 us
    unnamed x16, local copies, waits for them, and re-layouts  10.8 us
    dot_general x1, matrix products, body(): lax.dot_general(grad_full, down_weight, LAST_DIMS, preferred_element_type...  6.29 us
  transfers between devices with their start and end apart: 6, of which 6 were waited for; matrix products, arithmetic and copies ran while one was open for 12% of the time, Pallas kernels for 0%

profile of v1, /device:TPU:0, one launch (start us, length us, event | category | flops | bytes accessed | tf_op | source)
XLA Modules:
  0.0 313.5 jit_solution(16718450053814626498)
XLA Ops:
  7.2 0.7 all-gather.5.cloned.1.call-update
  7.9 0.0 reduce-scatter.3.cloned.1.call-start
  8.0 27.8 %all-gather.5.cloned.1.call-done = bf16[1024,512]{1,0:T(8,128)(2,1)} async-done(((bf16[128,512]{1,0:T(8,128)(2,1)}), bf16[1024,512]{1,0:T(8,128)(2,1)}) %all-gather.5.cloned.1.call-update) | async-done | bytes 1048592 | tf_op jit(solution)/shard_map/all_gather | solution.py:15
  35.8 6.3 %fusion.19 = f32[1024,1792]{1,0:T(8,128)} fusion(bf16[1024,512]{1,0:T(8,128)(2,1)} %all-gather.5.cloned.1.call-done, bf16[1792,512]{1,0:T(8,128)(2,1)S(1)} %copy-done), kind=kOutput, calls=%fused_computation.26 | convolution fusion | flops 1879048192 | bytes 10223616 | tf_op jit(solution)/shard_map/dot_general | solution.py:17
  42.1 0.0 all-gather.7.cloned.1.call-start
  42.2 82.8 %reduce-scatter.3.cloned.1.call-done = f32[64,1792]{1,0:T(8,128)} async-done(((f32[1024,1792]{1,0:T(8,128)}), f32[64,1792]{1,0:T(8,128)}) %reduce-scatter.3.cloned.1.call-update) | async-done | bytes 458768 | tf_op jit(solution)/shard_map/reduce_scatter | solution.py:20
  125.0 2.0 fusion.11
  127.0 0.8 pad_maximum_fusion
  127.8 0.0 all-gather.11.cloned.1.call-start
  127.8 0.5 all-gather.11.cloned.1.call-update
  128.4 0.5 all-gather.9.cloned.1.call-update
  129.0 0.0 reduce-scatter.5.cloned.1.call-start
  129.0 64.3 %all-gather.7.cloned.1.call-done = bf16[1024,3584]{1,0:T(8,128)(2,1)} async-done(((bf16[64,3584]{1,0:T(8,128)(2,1)}), bf16[1024,3584]{1,0:T(8,128)(2,1)}) %all-gather.7.cloned.1.call-update) | async-done | bytes 7340048 | tf_op jit(solution)/shard_map/all_gather | solution.py:30
  193.3 4.8 %fusion.1 = f32[1024,512]{1,0:T(8,128)S(1)} fusion(bf16[512,1792]{1,0:T(8,128)(2,1)} %param.12, bf16[1024,3584]{1,0:T(8,128)(2,1)} %all-gather.7.cloned.1.call-done), kind=kOutput, calls=%fused_computation.3 | convolution fusion | flops 1879048192 | bytes 7602176 | tf_op jit(solution)/shard_map/dot_general | solution.py:36
  198.1 0.4 copy-done.4
  198.5 3.5 %fusion.6 = f32[1024,512]{1,0:T(8,128)} fusion(f32[1024,512]{1,0:T(8,128)S(1)} %fusion.1, bf16[512,1792]{1,0:T(8,128)(2,1)S(1)} %copy-done.4, bf16[1024,3584]{1,0:T(8,128)(2,1)S(1)} %copy-done.3), kind=kOutput, calls=%fused_computation.8 | convolution fusion | flops 1879572480 | bytes 9699328 | tf_op jit(solution)/shard_map/dot_general | solution.py:34
  202.0 43.3 %all-gather.11.cloned.1.call-done = bf16[1024,1792]{1,0:T(8,128)(2,1)} async-done(((bf16[64,1792]{1,0:T(8,128)(2,1)}), bf16[1024,1792]{1,0:T(8,128)(2,1)}) %all-gather.11.cloned.1.call-update) | async-done | bytes 3670032 | tf_op jit(solution)/shard_map/all_gather | solution.py:16
  245.3 6.0 %fusion.20 = f32[1792,512]{1,0:T(8,128)} fusion(bf16[1024,1792]{1,0:T(8,128)(2,1)} %all-gather.11.cloned.1.call-done, bf16[1024,512]{1,0:T(8,128)(2,1)S(1)} %copy-done.5), kind=kOutput, calls=%fused_computation.27 | convolution fusion | flops 1879048192 | bytes 8388608 | tf_op jit(solution)/shard_map/dot_general | solution.py:26
  251.3 18.5 %all-gather.9.cloned.1.call-done = bf16[1024,512]{1,0:T(8,128)(2,1)} async-done(((bf16[128,512]{1,0:T(8,128)(2,1)}), bf16[1024,512]{1,0:T(8,128)(2,1)}) %all-gather.9.cloned.1.call-update) | async-done | bytes 1048592 | tf_op jit(solution)/shard_map/all_gather | solution.py:21
  269.8 6.3 %convolution_bitcast_fusion.1 = f32[512,1792]{0,1:T(8,128)} fusion(bf16[1024,512]{1,0:T(8,128)(2,1)} %all-gather.9.cloned.1.call-done, bf16[1024,3584]{1,0:T(8,128)(2,1)} %all-gather.7.cloned.1.call-done), kind=kOutput, calls=%fused_computation.1 | convolution fusion | flops 1879048192 | bytes 8388608 | tf_op jit(solution)/shard_map/dot_general | solution.py:41
  276.1 5.2 %copy.11 = f32[512,1792]{1,0:T(8,128)} copy(f32[512,1792]{0,1:T(8,128)} %convolution_bitcast_fusion.1) | data formatting | bytes 7340032
  281.3 6.1 %convolution_bitcast_fusion = f32[512,1792]{0,1:T(8,128)} fusion(bf16[1024,512]{1,0:T(8,128)(2,1)S(1)} %copy-done.6, bf16[1024,3584]{1,0:T(8,128)(2,1)} %all-gather.7.cloned.1.call-done), kind=kOutput, calls=%fused_computation | convolution fusion | flops 1879048192 | bytes 8388608 | tf_op jit(solution)/shard_map/dot_general | solution.py:42
  287.4 5.1 %copy.12 = f32[512,1792]{1,0:T(8,128)} copy(f32[512,1792]{0,1:T(8,128)} %convolution_bitcast_fusion) | data formatting | bytes 7340032
  292.5 14.1 %reduce-scatter.5.cloned.1.call-done = f32[128,512]{1,0:T(8,128)} async-done(((f32[1024,512]{1,0:T(8,128)}), f32[128,512]{1,0:T(8,128)}) %reduce-scatter.5.cloned.1.call-update) | async-done | bytes 262160 | tf_op jit(solution)/shard_map/reduce_scatter | solution.py:35
  (18 shorter events, 0.2 us)
Async XLA Ops:
  7.2 28.6 %copy-start = (bf16[1792,512]{1,0:T(8,128)(2,1)S(1)}, bf16[1792,512]{1,0:T(8,128)(2,1)}, u32[]{:S(2)}) copy-start(bf16[1792,512]{1,0:T(8,128)(2,1)} %param.13) | copy-start | bytes 5505028
  7.2 28.6 %all-gather.5.cloned.1.call-start = ((), (), s32[]{:S(2)}) async-start(), calls=%async_computation.2 | async-start | bytes 1179648 | tf_op jit(solution)/shard_map/all_gather | solution.py:15
  7.9 117.1 %reduce-scatter.3.cloned.1.call-start = ((), (), s32[]{:S(2)}) async-start(), calls=%async_computation.3 | async-start | bytes 7798784 | tf_op jit(solution)/shard_map/reduce_scatter | solution.py:20
  42.1 82.9 %copy-start.1 = (bf16[64,1792]{1,0:T(8,128)(2,1)S(1)}, bf16[64,1792]{1,0:T(8,128)(2,1)}, u32[]{:S(2)}) copy-start(bf16[64,1792]{1,0:T(8,128)(2,1)} %param.10) | copy-start | bytes 688132
  42.1 82.9 %copy-start.2 = (bf16[64,1792]{1,0:T(8,128)(2,1)S(1)}, bf16[64,1792]{1,0:T(8,128)(2,1)}, u32[]{:S(2)}) copy-start(bf16[64,1792]{1,0:T(8,128)(2,1)} %param.9) | copy-start | bytes 688132
  42.1 151.1 %all-gather.7.cloned.1.call-start = ((), (), s32[]{:S(2)}) async-start(), calls=%async_computation.4 | async-start | bytes 7798784 | tf_op jit(solution)/shard_map/all_gather | solution.py:30
  127.8 117.6 %all-gather.11.cloned.1.call-start = ((), (), s32[]{:S(2)}) async-start(), calls=%async_computation.7 | async-start | bytes 3899392 | tf_op jit(solution)/shard_map/all_gather | solution.py:16
  128.4 141.5 %all-gather.9.cloned.1.call-start = ((), (), s32[]{:S(2)}) async-start(), calls=%async_computation.6 | async-start | bytes 1179648 | tf_op jit(solution)/shard_map/all_gather | solution.py:21
  129.0 177.7 %reduce-scatter.5.cloned.1.call-start = ((), (), s32[]{:S(2)}) async-start(), calls=%async_computation.5 | async-start | bytes 2359296 | tf_op jit(solution)/shard_map/reduce_scatter | solution.py:35
  193.3 4.8 %copy-start.3 = (bf16[1024,3584]{1,0:T(8,128)(2,1)S(1)}, bf16[1024,3584]{1,0:T(8,128)(2,1)}, u32[]{:S(2)}) copy-start(bf16[1024,3584]{1,0:T(8,128)(2,1)} %all-gather.7.cloned.1.call-done) | copy-start | bytes 22020100
  193.3 5.2 %copy-start.4 = (bf16[512,1792]{1,0:T(8,128)(2,1)S(1)}, bf16[512,1792]{1,0:T(8,128)(2,1)}, u32[]{:S(2)}) copy-start(bf16[512,1792]{1,0:T(8,128)(2,1)} %param.11) | copy-start | bytes 5505028
  198.5 46.8 %copy-start.5 = (bf16[1024,512]{1,0:T(8,128)(2,1)S(1)}, bf16[1024,512]{1,0:T(8,128)(2,1)}, u32[]{:S(2)}) copy-start(bf16[1024,512]{1,0:T(8,128)(2,1)} %all-gather.5.cloned.1.call-done) | copy-start | bytes 3145732
  276.1 5.2 %copy-start.6 = (bf16[1024,512]{1,0:T(8,128)(2,1)S(1)}, bf16[1024,512]{1,0:T(8,128)(2,1)}, u32[]{:S(2)}) copy-start(bf16[1024,512]{1,0:T(8,128)(2,1)} %all-gather.9.cloned.1.call-done) | copy-start | bytes 3145732
Sparse Core Ops, SparseCore 0:
  9.7 26.0 all-gather.4
  42.2 82.6 reduce-scatter.2
  127.9 65.2 all-gather.6
  196.0 49.2 all-gather.10
  247.0 22.7 all-gather.8
  272.8 33.7 reduce-scatter.4
